TPU v7x, 256 devices: a whole 4x4x8 slice. The times are simulated.
256 devices in a mesh: ctx: 32 (over x, y, core), tp: 8 (over z).
Axes of the slice: x: 4, y: 4, z: 8, core: 2. Of those that a mesh axis runs over, the one named last changes fastest.
Arguments:
- resp_query: bfloat16 [2048, 4096], P('ctx', 'tp'), may hold values from -16 to 16, as said below
- resp_key: bfloat16 [2048, 2048], P('ctx', 'tp'), may hold values from -6 to 6
- resp_value: bfloat16 [2048, 2048], P('ctx', 'tp'), may hold values from -6 to 6
- prompt_key: bfloat16 [16384, 2048], P('ctx', 'tp'), may hold values from -6 to 6
- prompt_value: bfloat16 [16384, 2048], P('ctx', 'tp'), may hold values from -6 to 6
- o_weight: bfloat16 [4096, 4608], P('tp'), may hold values from -0.09375 to 0.09375
- d_hidden: bfloat16 [2048, 4608], P('ctx', 'tp'), may hold values from -6 to 6
- prompt_offsets: int32 [4], replicated, may hold values from 2048 to 16384, as said below
- resp_lengths: int32 [4], replicated, may hold values from 128 to 512, as said below
Outputs:
- attn_out: bfloat16 [2048, 4096], P('ctx', 'tp')
- hidden: bfloat16 [2048, 4608], P('ctx', 'tp')
- d_query: bfloat16 [2048, 4096], P('ctx', 'tp')
- d_prompt_key: bfloat16 [16384, 2048], P('ctx', 'tp')
- d_prompt_value: bfloat16 [16384, 2048], P('ctx', 'tp')
- d_resp_key: bfloat16 [2048, 2048], P('ctx', 'tp')
- d_resp_value: bfloat16 [2048, 2048], P('ctx', 'tp')
- d_o_weight: float32 [4096, 4608], P('tp', 'ctx')
Inputs may be any that keep to these rules, and one draw needn't show every extreme that they name: `resp_query`: response queries; every entry is finite. Response r follows the first prompt_offsets[r] prompt tokens; some response follows the whole prompt. Response r holds resp_lengths[r] real tokens at the start of its 512 rows; some response fills all of them.
All inputs are finite; a program needn't handle non-finite values.
Results may differ from a plain program's by a relative error of at most 0.03.
Values may be sent and summed in bfloat16 or wider, within the bound.
A program may use at most 128 MiB of HBM per device.

v0:
```python
import jax
import jax.numpy as jnp
from jax import lax
from jax.sharding import PartitionSpec as P

HD = 128
RESPONSES = 4
RESP_LEN = 512


SOFTCAP = 50.0
ATTN_SCALE = 144.0 ** (-0.5)


def response_table(row_ids, per_response):
    response_of = row_ids // RESP_LEN
    response_ids = jnp.arange(RESPONSES, dtype=jnp.int32)
    matches = response_of[:, None] == response_ids[None, :]
    return jnp.sum(jnp.where(matches, per_response[None, :], 0), axis=1)


def visibility(row_ids, prompt_pos, resp_rows, prompt_offsets, resp_lengths):
    response_of = row_ids // RESP_LEN
    position = row_ids % RESP_LEN
    offset_row = response_table(row_ids, prompt_offsets)
    length_row = response_table(row_ids, resp_lengths)
    key_response = resp_rows // RESP_LEN
    key_position = resp_rows % RESP_LEN
    see_prompt = (prompt_pos[None, :] >= 0) & (prompt_pos[None, :] < offset_row[:, None])
    see_own = (resp_rows[None, :] >= 0) & (key_response[None, :] == response_of[:, None])
    see_own = (
        see_own
        & (key_position[None, :] <= position[:, None])
        & (key_position[None, :] < length_row[:, None])
    )
    return see_prompt | see_own


def local_scores(query_four, key_three):
    raw_score = jnp.einsum(
        "qhgd,khd->hgqk", query_four, key_three, preferred_element_type=jnp.float32
    )
    return SOFTCAP * jnp.tanh(raw_score * ATTN_SCALE / SOFTCAP)


def local_forward(query_block, key_rows, value_rows, visible, kv_heads):
    row_count = query_block.shape[0]
    group_size = query_block.shape[1] // (kv_heads * HD)
    query_four = query_block.reshape(row_count, kv_heads, group_size, HD)
    key_three = key_rows.reshape(key_rows.shape[0], kv_heads, HD)
    value_three = value_rows.reshape(value_rows.shape[0], kv_heads, HD)
    scores = local_scores(query_four, key_three)
    weights = jnp.where(visible[None, None], jnp.exp(scores), 0.0)
    totals = jnp.sum(weights, axis=3).transpose(2, 0, 1).reshape(row_count, kv_heads * group_size)
    numerator = jnp.einsum(
        "hgqk,khd->qhgd",
        weights.astype(jnp.bfloat16),
        value_three,
        preferred_element_type=jnp.float32,
    )
    return (numerator.reshape(row_count, query_block.shape[1]), totals)


def local_backward(
    query_block, grad_block, total_block, delta_block, key_rows, value_rows, visible, kv_heads
):
    row_count = query_block.shape[0]
    group_size = query_block.shape[1] // (kv_heads * HD)
    query_four = query_block.reshape(row_count, kv_heads, group_size, HD)
    grad_four = grad_block.reshape(row_count, kv_heads, group_size, HD)
    key_three = key_rows.reshape(key_rows.shape[0], kv_heads, HD)
    value_three = value_rows.reshape(value_rows.shape[0], kv_heads, HD)
    scores = local_scores(query_four, key_three)
    weights = jnp.where(visible[None, None], jnp.exp(scores), 0.0)
    totals_four = total_block.reshape(row_count, kv_heads, group_size).transpose(1, 2, 0)[..., None]
    delta_four = delta_block.reshape(row_count, kv_heads, group_size).transpose(1, 2, 0)[..., None]
    probs = weights / totals_four
    prob_grad = jnp.einsum(
        "qhgd,khd->hgqk", grad_four, value_three, preferred_element_type=jnp.float32
    )
    capped = 1.0 - scores / SOFTCAP * (scores / SOFTCAP)
    score_grad = (probs * (prob_grad - delta_four) * capped * ATTN_SCALE).astype(jnp.bfloat16)
    query_grad = jnp.einsum(
        "hgqk,khd->qhgd", score_grad, key_three, preferred_element_type=jnp.float32
    )
    key_grad = jnp.einsum(
        "hgqk,qhgd->khd", score_grad, query_four, preferred_element_type=jnp.float32
    )
    value_grad = jnp.einsum(
        "hgqk,qhgd->khd", probs.astype(jnp.bfloat16), grad_four, preferred_element_type=jnp.float32
    )
    return (
        query_grad.reshape(row_count, query_block.shape[1]),
        key_grad.reshape(key_rows.shape),
        value_grad.reshape(value_rows.shape),
    )


def per_device(
    resp_query,
    resp_key,
    resp_value,
    prompt_key,
    prompt_value,
    o_weight,
    d_hidden,
    prompt_offsets,
    resp_lengths,
):
    ctx_index = lax.axis_index("ctx")
    own_count = resp_query.shape[0]
    prompt_count = prompt_key.shape[0]
    query_cols = resp_query.shape[1]
    kv_cols = prompt_key.shape[1]
    kv_heads = kv_cols // HD
    q_heads = query_cols // HD
    key_rows = jnp.concatenate([prompt_key, resp_key], 0)
    value_rows = jnp.concatenate([prompt_value, resp_value], 0)
    key_count = prompt_count + own_count
    key_slots = jnp.arange(key_count, dtype=jnp.int32)
    prompt_pos = jnp.where(key_slots < prompt_count, ctx_index * prompt_count + key_slots, -1)
    resp_rows = jnp.where(
        key_slots >= prompt_count, ctx_index * own_count + key_slots - prompt_count, -1
    )
    block_ids = jnp.arange(RESPONSES, dtype=jnp.int32)

    def block_visible(block_id):
        row_ids = block_id * RESP_LEN + jnp.arange(RESP_LEN, dtype=jnp.int32)
        return visibility(row_ids, prompt_pos, resp_rows, prompt_offsets, resp_lengths)

    all_queries = lax.all_gather(resp_query, "ctx", axis=0, tiled=True)

    def forward_block(running, operands):
        block_id, query_block = operands
        visible = block_visible(block_id)
        outcome = local_forward(query_block, key_rows, value_rows, visible, kv_heads)
        return (running, outcome)

    _, (numerators, totals) = lax.scan(
        forward_block,
        jnp.int32(0),
        (block_ids, all_queries.reshape(RESPONSES, RESP_LEN, query_cols)),
    )
    total_rows = numerators.shape[0] * RESP_LEN
    all_totals = lax.psum(totals.reshape(total_rows, q_heads), "ctx")
    shares = numerators.reshape(total_rows, q_heads, HD) / all_totals[:, :, None]
    own_merged = lax.psum_scatter(
        shares.reshape(total_rows, query_cols), "ctx", scatter_dimension=0, tiled=True
    )
    own_ids = ctx_index * own_count + jnp.arange(own_count, dtype=jnp.int32)
    valid = own_ids % RESP_LEN < response_table(own_ids, resp_lengths)
    attn_out = jnp.where(valid[:, None], own_merged, 0.0).astype(jnp.bfloat16)
    hidden_part = jnp.dot(attn_out, o_weight, preferred_element_type=jnp.float32)
    hidden = lax.psum_scatter(hidden_part, "tp", scatter_dimension=1, tiled=True).astype(
        jnp.bfloat16
    )
    full_grad = lax.all_gather(d_hidden, "tp", axis=1, tiled=True)
    grad_out = jnp.dot(full_grad, o_weight.T, preferred_element_type=jnp.float32).astype(
        jnp.bfloat16
    )
    grad_out = jnp.where(valid[:, None], grad_out, jnp.zeros_like(grad_out))
    row_delta = jnp.sum(
        grad_out.astype(jnp.float32).reshape(own_count, q_heads, HD)
        * attn_out.astype(jnp.float32).reshape(own_count, q_heads, HD),
        axis=2,
    )
    all_grad = lax.all_gather(grad_out, "ctx", axis=0, tiled=True)
    all_delta = lax.all_gather(row_delta, "ctx", axis=0, tiled=True)

    def backward_block(running, operands):
        block_id, query_block, grad_block, total_block, delta_block = operands
        visible = block_visible(block_id)
        outcome = local_backward(
            query_block,
            grad_block,
            total_block,
            delta_block,
            key_rows,
            value_rows,
            visible,
            kv_heads,
        )
        query_grad, key_grad, value_grad = outcome
        return ((running[0] + key_grad, running[1] + value_grad), query_grad)

    initial = (
        jnp.zeros((key_count, kv_cols), jnp.float32),
        jnp.zeros((key_count, kv_cols), jnp.float32),
    )
    (key_grads, value_grads), query_terms = lax.scan(
        backward_block,
        initial,
        (
            block_ids,
            all_queries.reshape(RESPONSES, RESP_LEN, query_cols),
            all_grad.reshape(RESPONSES, RESP_LEN, query_cols),
            all_totals.reshape(RESPONSES, RESP_LEN, q_heads),
            all_delta.reshape(RESPONSES, RESP_LEN, q_heads),
        ),
    )
    d_query = lax.psum_scatter(
        query_terms.reshape(-1, query_cols), "ctx", scatter_dimension=0, tiled=True
    ).astype(jnp.bfloat16)
    key_grads = key_grads.astype(jnp.bfloat16)
    value_grads = value_grads.astype(jnp.bfloat16)
    weight_terms = lax.dot_general(
        attn_out, full_grad, (((0,), (0,)), ((), ())), preferred_element_type=jnp.float32
    )
    d_o_weight = lax.psum_scatter(weight_terms, "ctx", scatter_dimension=1, tiled=True)
    return (
        attn_out,
        hidden,
        d_query,
        key_grads[:prompt_count],
        value_grads[:prompt_count],
        key_grads[prompt_count:],
        value_grads[prompt_count:],
        d_o_weight,
    )


def solution(mesh):
    in_specs = (
        P("ctx", "tp"),
        P("ctx", "tp"),
        P("ctx", "tp"),
        P("ctx", "tp"),
        P("ctx", "tp"),
        P("tp", None),
        P("ctx", "tp"),
        P(),
        P(),
    )
    out_specs = (
        P("ctx", "tp"),
        P("ctx", "tp"),
        P("ctx", "tp"),
        P("ctx", "tp"),
        P("ctx", "tp"),
        P("ctx", "tp"),
        P("ctx", "tp"),
        P("tp", "ctx"),
    )
    return jax.shard_map(
        per_device, mesh=mesh, in_specs=in_specs, out_specs=out_specs, check_vma=False
    )
```

profile of v0, /device:TPU:2, one launch (start us, length us, event | category | flops | bytes accessed | tf_op | source)
XLA Modules:
  0.0 638.9 jit_solution(2445905862251511902)
XLA Ops:
  10.9 51.1 %all-gather.5.cloned.1.call-done = bf16[2048,512]{1,0:T(8,128)(2,1)} async-done(((bf16[64,512]{1,0:T(8,128)(2,1)}), bf16[2048,512]{1,0:T(8,128)(2,1)}) %all-gather.5.cloned.1.call-update) | async-done | bytes 2097168 | tf_op jit(solution)/shard_map/all_gather | solution.py:131
  62.0 4.1 copy.96
  66.1 2.5 broadcast.938.clone2
  68.6 31.9 %while.41 = (s32[]{:T(128)}, f32[4,512,512]{2,1,0:T(8,128)}, f32[4,512,4]{1,2,0:T(4,128)S(1)}, s32[4]{0:T(128)S(1)}, s32[4]{0:T(128)S(1)}, /*index=5*/s32[4]{0:T...) while((s32[]{:T(128)}, f32[4,512,512]{2,1,0:T(8,128)}, ...), condition=%wide.wide.region_5.6_spmd.clone.clone, body=%wide.wide.region_1.5_spmd.clone.clone.sunk | while | flops 616116800 | bytes 17809012 | solution.py:139
  100.5 109.1 %psum.7 = f32[2048,4]{0,1:T(4,128)S(1)} all-reduce(f32[2048,4]{0,1:T(4,128)S(1)} %bitcast.214), channel_id=1, replica_groups=mesh['ctx'=32,'tp'=8] {'ctx'}, use_global_device_ids=true, to_apply=%region_6.7 | all-reduce | flops 8192 | bytes 65536 | tf_op jit(solution)/shard_map/psum | solution.py:145
  209.9 4.7 div.109
  214.6 3.0 bitcast_divide_fusion.1
  217.7 27.2 %all-gather = bf16[8,576,64]{1,2,0:T(8,128)(2,1)S(1)} all-gather(bf16[1,576,64]{1,2,0:T(8,128)(2,1)S(1)} %bitcast.213), channel_id=1, replica_groups=mesh['ctx'=32,'tp'=8] {'tp'}, dimensions={0}, use_global_device_ids=true | all-gather | bytes 663552 | tf_op jit(solution)/shard_map/all_gather | solution.py:157
  245.8 75.2 %reduce-scatter.7.cloned.1.call-done = f32[64,512]{1,0:T(8,128)} async-done(((f32[2048,512]{1,0:T(8,128)}), f32[64,512]{1,0:T(8,128)}) %reduce-scatter.7.cloned.1.call-update) | async-done | bytes 131088 | tf_op jit(solution)/shard_map/reduce_scatter | solution.py:147
  321.1 4.5 convert_multiply_fusion
  326.1 22.7 %all-gather.1 = f32[32,64,4]{1,2,0:T(4,128)S(1)} all-gather(f32[1,64,4]{1,2,0:T(4,128)S(1)} %copy.100), channel_id=1, replica_groups=mesh['ctx'=32,'tp'=8] {'ctx'}, dimensions={0}, use_global_device_ids=true | all-gather | bytes 33792 | tf_op jit(solution)/shard_map/all_gather | solution.py:168
  348.9 5.7 convolution_bitcast_fusion.1
  354.6 19.2 %all-gather.7.cloned.1.call-done = bf16[2048,512]{1,0:T(8,128)(2,1)} async-done(((bf16[64,512]{1,0:T(8,128)(2,1)}), bf16[2048,512]{1,0:T(8,128)(2,1)}) %all-gather.7.cloned.1.call-update) | async-done | bytes 2097168 | tf_op jit(solution)/shard_map/all_gather | solution.py:167
  373.9 2.6 broadcast.938.clone
  376.5 59.4 %while.42 = (s32[]{:T(128)}, f32[576,256]{1,0:T(8,128)}, f32[576,256]{1,0:T(8,128)S(1)}, f32[4,512,512]{2,1,0:T(8,128)}, bf16[4,512,512]{1,2,0:T(8,128)(2,1)}, /...) while((s32[]{:T(128)}, f32[576,256]{1,0:T(8,128)}, ...), condition=%wide.wide.region_13.14_spmd.clone.clone.clone, body=%wide.wide.region_10.13_spmd.clone.clone.clone.sunk | while | flops 1532122496 | bytes 38338228 | solution.py:190
  383.6 2.9 fusion.134
  397.6 2.9 fusion.134
  401.9 2.3 bitcast_add_fusion.4
  412.7 2.9 fusion.134
  417.0 2.3 bitcast_add_fusion.4
  427.7 2.9 fusion.134
  435.9 6.1 fusion.65
  447.6 77.4 %reduce-scatter.9.cloned.1.call-done = f32[64,512]{1,0:T(8,128)} async-done(((f32[2048,512]{1,0:T(8,128)}), f32[64,512]{1,0:T(8,128)}) %reduce-scatter.9.cloned.1.call-update) | async-done | bytes 131088 | tf_op jit(solution)/shard_map/reduce_scatter | solution.py:201
  526.5 105.5 %reduce-scatter.11.cloned.1.call-done = f32[512,144]{0,1:T(8,128)} async-done(((f32[512,4608]{0,1:T(8,128)}), f32[512,144]{0,1:T(8,128)}) %reduce-scatter.11.cloned.1.call-update) | async-done | bytes 294928 | tf_op jit(solution)/shard_map/reduce_scatter | solution.py:209
  (230 shorter events, 81.9 us)
Async XLA Ops:
  7.2 54.8 %all-gather.5.cloned.1.call-start = ((), (), s32[]{:S(2)}) async-start(), calls=%async_computation.4 | async-start | bytes 2162688 | tf_op jit(solution)/shard_map/all_gather | solution.py:131
  7.9 313.2 %reduce-scatter.7.cloned.1.call-start = ((), (), s32[]{:S(2)}) async-start(), calls=%async_computation.5 | async-start | bytes 4325376 | tf_op jit(solution)/shard_map/reduce_scatter | solution.py:147
  10.7 57.9 %copy-start.2 = (bf16[576,256]{1,0:T(8,128)(2,1)}, bf16[576,256]{1,0:T(8,128)(2,1)S(1)}, u32[]{:S(2)}) copy-start(bf16[576,256]{1,0:T(8,128)(2,1)S(1)} %get-tuple-element.1349) | copy-start | bytes 884740
  10.7 57.9 %copy-start.4 = (bf16[576,256]{1,0:T(8,128)(2,1)}, bf16[576,256]{1,0:T(8,128)(2,1)S(1)}, u32[]{:S(2)}) copy-start(bf16[576,256]{1,0:T(8,128)(2,1)S(1)} %get-tuple-element.1352) | copy-start | bytes 884740
  10.7 57.9 %copy-start.8 = (s32[4]{0:T(128)S(1)}, s32[4]{0:T(128)}, u32[]{:S(2)}) copy-start(s32[4]{0:T(128)} %param.20) | copy-start | bytes 52
  10.7 57.9 %copy-start.9 = (s32[4]{0:T(128)S(1)}, s32[4]{0:T(128)}, u32[]{:S(2)}) copy-start(s32[4]{0:T(128)} %param.21) | copy-start | bytes 52
  209.9 4.7 copy-start
  214.6 3.1 copy-start.7
  217.6 108.1 %copy-start.3 = (bf16[576,256]{1,0:T(8,128)(2,1)S(1)}, bf16[576,256]{1,0:T(8,128)(2,1)}, u32[]{:S(2)}) copy-start(bf16[576,256]{1,0:T(8,128)(2,1)} %get-tuple-element.1416) | copy-start | bytes 884740
  217.6 156.3 %all-gather.7.cloned.1.call-start = ((), (), s32[]{:S(2)}) async-start(), calls=%async_computation.6 | async-start | bytes 2162688 | tf_op jit(solution)/shard_map/all_gather | solution.py:167
  217.7 108.1 %copy-start.5 = (bf16[576,256]{1,0:T(8,128)(2,1)S(1)}, bf16[576,256]{1,0:T(8,128)(2,1)}, u32[]{:S(2)}) copy-start(bf16[576,256]{1,0:T(8,128)(2,1)} %get-tuple-element.1417) | copy-start | bytes 884740
  245.7 80.0 %copy-start.1 = (bf16[4608,64]{0,1:T(8,128)(2,1)}, bf16[4608,64]{0,1:T(8,128)(2,1)S(1)}, u32[]{:S(2)}) copy-start(bf16[4608,64]{0,1:T(8,128)(2,1)S(1)} %reshape.676) | copy-start | bytes 1769476
  325.6 110.3 %copy-start.6 = (bf16[64,512]{1,0:T(8,128)(2,1)}, bf16[64,512]{1,0:T(8,128)(2,1)S(1)}, u32[]{:S(2)}) copy-start(bf16[64,512]{1,0:T(8,128)(2,1)S(1)} %get-tuple-element.956) | copy-start | bytes 196612
  325.6 116.5 %reduce-scatter.13.cloned.1.call-start = ((), (), s32[]{:S(2)}) async-start(), calls=%async_computation.9 | async-start | bytes 2654208
  354.6 170.4 %reduce-scatter.9.cloned.1.call-start = ((), (), s32[]{:S(2)}) async-start(), calls=%async_computation.7 | async-start | bytes 4325376 | tf_op jit(solution)/shard_map/reduce_scatter | solution.py:201
  435.9 196.2 %reduce-scatter.11.cloned.1.call-start = ((), (), s32[]{:S(2)}) async-start(), calls=%async_computation.8 | async-start | bytes 9732096 | tf_op jit(solution)/shard_map/reduce_scatter | solution.py:209
Sparse Core Ops, SparseCore 0:
  10.6 51.3 all-gather.4
  217.7 103.2 reduce-scatter.6
  325.7 48.1 all-gather.6
  376.5 42.8 reduce-scatter.12
  436.0 88.9 reduce-scatter.8
  529.5 102.5 reduce-scatter.10
where the time goes:
time: 640 us; the launch traced here: 639 us
  waiting for transfers between devices  329 us (51%)
  blocking collectives  159 us (25%)
  matrix products  55.2 us (9%)
  local copies, waits for them, and re-layouts  52.9 us (8%)
  other arithmetic  22.1 us (3%)
  between operations  14.4 us (2%)
    psum x1, blocking collectives, per_device(): all_totals = lax.psum(totals.reshape(total_rows, q_heads), 'ctx')  109 us
    reduce_scatter x1, waiting for transfers between devices, per_device(): lax.psum_scatter(weight_terms, 'ctx', scatter_dimension=1, tiled=True)  105 us
    reduce_scatter x1, waiting for transfers between devices, per_device(): lax.psum_scatter(query_terms.reshape(-1, query_cols), 'ctx', scatter_dime...  77.4 us
    reduce_scatter x1, waiting for transfers between devices, per_device(): lax.psum_scatter(shares.reshape(total_rows, query_cols), 'ctx', scatter_d...  75.2 us
    all_gather x1, waiting for transfers between devices, per_device(): all_queries = lax.all_gather(resp_query, 'ctx', axis=0, tiled=True)  51.1 us
    all_gather x1, blocking collectives, per_device(): full_grad = lax.all_gather(d_hidden, 'tp', axis=1, tiled=True)  27.2 us
    all_gather x1, blocking collectives, per_device(): all_delta = lax.all_gather(row_delta, 'ctx', axis=0, tiled=True)  22.7 us
    all_gather x1, waiting for transfers between devices, per_device(): all_grad = lax.all_gather(grad_out, 'ctx', axis=0, tiled=True)  19.2 us
  transfers between devices with their start and end apart: 6, of which 5 were waited for; matrix products, arithmetic and copies ran while one was open for 13% of the time, Pallas kernels for 0%

commit v1 on v0

v1 whole, which is shorter than its diff:
```python
import math

import jax
import jax.numpy as jnp
from jax import lax
from jax.experimental import pallas as pl
from jax.experimental.pallas import tpu as pltpu
from jax.sharding import PartitionSpec as P

F32 = jnp.float32
BF16 = jnp.bfloat16
MESH = pl.DeviceIdType.MESH

NX, NY, NZ = 4, 4, 8
CHIPS = NX * NY
PAIRS = CHIPS // 2
HD = 128
ROWS = 64
PKEYS = 1024
RKEYS = 128
KEYS = PKEYS + RKEYS
CHUNK = 256
WIDTH = 4608
ZCOLS = WIDTH // NZ
JCOLS = WIDTH // CHIPS
DCOLS = JCOLS // 2
QCOLS = 512

TANH_IN = 1.0 / 600.0
EXP_IN = 50.0 * math.log2(math.e)


def dot_nt(a, b):
    return lax.dot_general(a, b, (((1,), (1,)), ((), ())), preferred_element_type=F32)


def dot_nn(a, b):
    return lax.dot_general(a, b, (((1,), (0,)), ((), ())), preferred_element_type=F32)


def dot_tn(a, b):
    return lax.dot_general(a, b, (((0,), (0,)), ((), ())), preferred_element_type=F32)


def transpose(a):
    return jnp.swapaxes(a, 0, 1)


def kernel(
    off_ref, len_ref, q_ref, dh_ref, rk_hbm, rv_hbm, pk_hbm, pv_hbm, ow_hbm,
    attn_out, hidden_out, dq_out, dpk_out, dpv_out, drk_out, drv_out, dow_out,
    qall, doall, kbuf, vbuf, kT, vT, wbuf, gbuf, wresp, gresp,
    osend, orecv, stall, atall, dhg, dfull, dhall, ow, hp, hsend, hrecv,
    dqsend, dqrecv, dkacc, dvacc, gsend, grecv, dowsend, dowrecv, oacc, dqacc,
    q_s, q_r, do_s, do_r, o_s, o_r, st_s, st_r, at_s, at_r, dh_s, dh_r, dq_s, dq_r,
    zg_s, zg_r, h_s, h_r, kv_l, kv_s, kv_r, ow_l, g_s, g_r, dw_s, dw_r,
):
    c = lax.axis_index("ctx")
    z = lax.axis_index("tp")
    core = lax.rem(c, 2)
    chip = lax.div(c, 2)
    x = lax.div(chip, NY)
    y = lax.rem(chip, NY)
    sibling = chip * 2 + 1 - core

    def peer_chip(s):
        px = lax.rem(x + lax.div(s, NY), NX)
        py = lax.rem(y + lax.rem(s, NY), NY)
        return px * NY + py

    def back(s):
        bx = lax.rem(NX - lax.div(s, NY), NX)
        by = lax.rem(NY - lax.rem(s, NY), NY)
        return bx * NY + by

    def plane_copy(src, dst_buf, send, recv, s):
        return pltpu.make_async_remote_copy(
            src_ref=src, dst_ref=dst_buf.at[back(s)], send_sem=send.at[s], recv_sem=recv.at[back(s)],
            device_id=(peer_chip(s) * 2 + core, z), device_id_type=MESH)

    def plane_wait_recv(src, buf, send, recv, s):
        pltpu.make_async_remote_copy(
            src_ref=src, dst_ref=buf.at[s], send_sem=send.at[s], recv_sem=recv.at[s],
            device_id=(peer_chip(s) * 2 + core, z), device_id_type=MESH).wait_recv()

    def z_copy(src, dst, send, recv, dz):
        return pltpu.make_async_remote_copy(
            src_ref=src, dst_ref=dst, send_sem=send.at[dz], recv_sem=recv.at[z],
            device_id=(c, lax.rem(z + dz, NZ)), device_id_type=MESH)

    own_p = pl.multiple_of(core * 512, 512)
    own_r = pl.multiple_of(PKEYS + core * ROWS, ROWS)

    def kv_pieces():
        pieces = []
        for h in range(2):
            cols = pl.ds(HD * h, HD)
            pieces.append((pk_hbm.at[:, cols], kbuf.at[h, pl.ds(own_p, 512)]))
            pieces.append((pv_hbm.at[:, cols], vbuf.at[h, pl.ds(own_p, 512)]))
            pieces.append((rk_hbm.at[:, cols], kbuf.at[h, pl.ds(own_r, ROWS)]))
            pieces.append((rv_hbm.at[:, cols], vbuf.at[h, pl.ds(own_r, ROWS)]))
        return pieces

    sib_p = pl.multiple_of(512 - core * 512, 512)
    sib_r = pl.multiple_of(PKEYS + ROWS - core * ROWS, ROWS)

    def kv_landing():
        places = []
        for h in range(2):
            places.append(kbuf.at[h, pl.ds(sib_p, 512)])
            places.append(vbuf.at[h, pl.ds(sib_p, 512)])
            places.append(kbuf.at[h, pl.ds(sib_r, ROWS)])
            places.append(vbuf.at[h, pl.ds(sib_r, ROWS)])
        return places

    for n, (src, dst) in enumerate(kv_pieces()):
        pltpu.make_async_copy(src, dst, kv_l.at[n]).start()
    ow_load = pltpu.make_async_copy(ow_hbm, ow, ow_l)
    ow_load.start()

    for h in range(2):
        for g in range(2):
            qall[0, h, g * ROWS:(g + 1) * ROWS, :] = q_ref[:, (2 * h + g) * HD:(2 * h + g + 1) * HD]
    dh_own = dh_ref[...].astype(F32)
    for half in range(2):
        dhg[2 * z + half] = dh_own[:, half * JCOLS:(half + 1) * JCOLS].astype(BF16)

    barrier = pltpu.get_barrier_semaphore()

    def greet_plane(s, carry):
        pl.semaphore_signal(barrier, inc=1, device_id=(peer_chip(s) * 2 + core, z), device_id_type=MESH)
        return carry

    def greet_z(dz, carry):
        pl.semaphore_signal(barrier, inc=1, device_id=(c, lax.rem(z + dz, NZ)), device_id_type=MESH)
        return carry

    lax.fori_loop(1, CHIPS, greet_plane, 0)
    lax.fori_loop(1, NZ, greet_z, 0)
    pl.semaphore_signal(barrier, inc=1, device_id=(sibling, z), device_id_type=MESH)
    pl.semaphore_wait(barrier, CHIPS - 1 + NZ - 1 + 1)

    for n, (src, dst) in enumerate(kv_pieces()):
        pltpu.make_async_remote_copy(
            src_ref=src, dst_ref=dst, send_sem=kv_s.at[n], recv_sem=kv_r.at[n],
            device_id=(sibling, z), device_id_type=MESH).start()

    def send_q(s, carry):
        plane_copy(qall.at[0], qall, q_s, q_r, s).start()
        return carry

    lax.fori_loop(1, CHIPS, send_q, 0)

    def send_dh(dz, carry):
        block = dhg.at[pl.ds(2 * z, 2)]
        z_copy(block, block, zg_s, zg_r, dz).start()
        return carry

    lax.fori_loop(1, NZ, send_dh, 0)

    dkacc[...] = jnp.zeros_like(dkacc)
    dvacc[...] = jnp.zeros_like(dvacc)
    for n, (src, dst) in enumerate(kv_pieces()):
        pltpu.make_async_copy(src, dst, kv_l.at[n]).wait()
    for n, dst in enumerate(kv_landing()):
        pltpu.make_async_remote_copy(
            src_ref=dst, dst_ref=dst, send_sem=kv_s.at[n], recv_sem=kv_r.at[n],
            device_id=(sibling, z), device_id_type=MESH).wait_recv()
    for h in range(2):
        vT[h, HD:, :] = jnp.ones((16, KEYS), BF16)
        for n in range(KEYS // HD):
            rows = pl.ds(n * HD, HD)
            kT[h, :, rows] = transpose(kbuf[h, rows, :])
            vT[h, 0:HD, rows] = transpose(vbuf[h, rows, :])

    sub = lax.broadcasted_iota(jnp.int32, (CHUNK, 2 * HD), 0)

    def weigh(s, mask):
        t = jnp.tanh(s * TANH_IN)
        w = jnp.exp2(t * EXP_IN)
        w = jnp.where(mask, w, 0.0)
        return w.astype(BF16), (w * (1.0 - t * t)).astype(BF16)

    def emit_o(i, h, acc):
        tot = acc[HD:, :]
        rest = tot - tot.astype(BF16).astype(F32)
        row = lax.broadcasted_iota(jnp.int32, tot.shape, 0)
        tail = jnp.where(row < 8, tot, rest).astype(BF16)
        head = acc[:HD, :].astype(BF16)
        for e in range(2):
            lanes = slice(e * HD, (e + 1) * HD)
            osend[2 * i + e, h, 0:HD, :] = head[:, lanes]
            osend[2 * i + e, h, HD:, :] = tail[:, lanes]

    def wait_q(s):
        plane_wait_recv(qall.at[0], qall, q_s, q_r, s)

    def send_o(s):
        plane_copy(osend.at[s], orecv, o_s, o_r, s).start()

    def forward_step(i, carry):
        @pl.when(i > 0)
        def _():
            wait_q(2 * i)

        wait_q(2 * i + 1)
        limit = off_ref[lax.rem(x + lax.div(i, 2), NX)] - chip * PKEYS
        for h in range(2):
            q2 = qall[pl.ds(2 * i, 2), h].reshape(2 * HD, HD)
            acc = jnp.zeros((HD + 16, 2 * HD), F32)
            for n in range(PKEYS // CHUNK):
                rows = slice(n * CHUNK, (n + 1) * CHUNK)
                wb, gb = weigh(dot_nt(kbuf[h, rows, :], q2), sub < limit - n * CHUNK)
                wbuf[i, h, rows, :] = wb
                gbuf[i, h, rows, :] = gb
                acc = acc + dot_nn(vT[h, :, rows], wb)
            oacc[h] = acc

        @pl.when(i < 2)
        def _():
            length = len_ref[x]
            lane = lax.broadcasted_iota(jnp.int32, (RKEYS, 2 * HD), 1)
            key = lax.broadcasted_iota(jnp.int32, (RKEYS, 2 * HD), 0) + y * RKEYS
            first = lax.rem(y + 2 * i, NY) * RKEYS + core * ROWS
            second = lax.rem(y + 2 * i + 1, NY) * RKEYS + core * ROWS
            row = lax.rem(lane, ROWS) + jnp.where(lane < HD, first, second)
            mask = (key <= row) & (key < length)
            for h in range(2):
                q2 = qall[pl.ds(2 * i, 2), h].reshape(2 * HD, HD)
                wb, gb = weigh(dot_nt(kbuf[h, PKEYS:, :], q2), mask)
                wresp[i, h] = wb
                gresp[i, h] = gb
                oacc[h] = oacc[h] + dot_nn(vT[h, :, PKEYS:], wb)

        for h in range(2):
            emit_o(i, h, oacc[h])

        @pl.when(i > 0)
        def _():
            send_o(2 * i)

        send_o(2 * i + 1)
        return carry

    lax.fori_loop(0, PAIRS, forward_step, 0)

    def wait_dh(dz, carry):
        src = lax.rem(z + dz, NZ)
        block = dhg.at[pl.ds(2 * src, 2)]
        pltpu.make_async_remote_copy(
            src_ref=block, dst_ref=block, send_sem=zg_s.at[dz], recv_sem=zg_r.at[src],
            device_id=(c, src), device_id_type=MESH).wait_recv()
        return carry

    lax.fori_loop(1, NZ, wait_dh, 0)

    def send_dh2(s, carry):
        plane_copy(dhg.at[peer_chip(s)], dhall, dh_s, dh_r, s).start()
        return carry

    for j in range(CHIPS):
        dfull[:, j * JCOLS:(j + 1) * JCOLS] = dhg[j].astype(F32)
    ow_load.wait()
    position = y * RKEYS + core * ROWS
    grad = dot_nt(dfull[...].astype(BF16), ow[...])
    row_at = lax.broadcasted_iota(jnp.int32, (ROWS, QCOLS), 0) + position
    grad = jnp.where(row_at < len_ref[x], grad, 0.0).astype(BF16)
    for h in range(2):
        for g in range(2):
            doall[0, h, g * ROWS:(g + 1) * ROWS, :] = grad[:, (2 * h + g) * HD:(2 * h + g + 1) * HD]

    def send_do(s, carry):
        plane_copy(doall.at[0], doall, do_s, do_r, s).start()
        return carry

    lax.fori_loop(1, CHIPS, send_do, 0)

    def merge(s, total):
        plane_wait_recv(osend.at[s], orecv, o_s, o_r, s)
        return total + orecv[s].astype(F32)

    merged = lax.fori_loop(1, CHIPS, merge, osend[0].astype(F32))
    lane = lax.broadcasted_iota(jnp.int32, (HD, HD), 1)
    valid = lax.rem(lane, ROWS) + position < len_ref[x]
    stall[0] = jnp.zeros((8, HD), F32)
    for h in range(2):
        total = merged[h, HD:HD + 1, :] + merged[h, HD + 8:HD + 9, :]
        inv = 1.0 / total
        own = jnp.where(valid, merged[h, 0:HD, :] * inv, 0.0).astype(BF16).astype(F32)
        grad_t = transpose(doall[0, h].astype(F32))
        delta = jnp.sum(own * grad_t, axis=0, keepdims=True)
        stall[0, 2 * h:2 * h + 1, :] = inv
        stall[0, 2 * h + 1:2 * h + 2, :] = delta * inv
        rows_first = transpose(own)
        for g in range(2):
            atall[0, :, (2 * h + g) * HD:(2 * h + g + 1) * HD] = rows_first[g * ROWS:(g + 1) * ROWS, :].astype(BF16)

    def send_st(s, carry):
        plane_copy(stall.at[0], stall, st_s, st_r, s).start()
        return carry

    def send_at(s, carry):
        plane_copy(atall.at[0], atall, at_s, at_r, s).start()
        return carry

    lax.fori_loop(1, CHIPS, send_st, 0)
    lax.fori_loop(1, CHIPS, send_at, 0)
    lax.fori_loop(1, CHIPS, send_dh2, 0)
    attn_out[...] = atall[0]

    hp[...] = dot_nn(atall[0], ow[...])
    for n in range(NZ):
        hsend[n] = hp[:, n * ZCOLS:(n + 1) * ZCOLS].astype(BF16)

    def send_h(dz, carry):
        z_copy(hsend.at[lax.rem(z + dz, NZ)], hrecv.at[z], h_s, h_r, dz).start()
        return carry

    lax.fori_loop(1, NZ, send_h, 0)

    def send_dq(s):
        plane_copy(dqsend.at[s], dqrecv, dq_s, dq_r, s).start()

    def wait_stats(s):
        plane_wait_recv(doall.at[0], doall, do_s, do_r, s)
        plane_wait_recv(stall.at[0], stall, st_s, st_r, s)

    def scaled_grad(i, h):
        parts, deltas = [], []
        for e in range(2):
            inv = stall[2 * i + e, 2 * h:2 * h + 1, :]
            inv = transpose(jnp.broadcast_to(inv, (HD, HD)))
            parts.append((doall[2 * i + e, h].astype(F32) * inv).astype(BF16))
            deltas.append(stall[2 * i + e, 2 * h + 1:2 * h + 2, :])
        return jnp.concatenate(parts, axis=0), jnp.concatenate(deltas, axis=1)

    def back_chunk(h, rows, wb, gb, q2, do2, delta):
        dp = dot_nt(vbuf[h, rows, :], do2)
        ds = (gb.astype(F32) * (dp - delta)).astype(BF16)
        dkacc[h, rows, :] += dot_nn(ds, q2)
        dvacc[h, rows, :] += dot_nn(wb, do2)
        return dot_nn(kT[h, :, rows], ds)

    def emit_dq(i, h, acc):
        for e in range(2):
            dqsend[2 * i + e, h] = acc[:, e * HD:(e + 1) * HD].astype(BF16)

    def backward_step(i, carry):
        @pl.when(i > 0)
        def _():
            wait_stats(2 * i)

        wait_stats(2 * i + 1)
        for h in range(2):
            q2 = qall[pl.ds(2 * i, 2), h].reshape(2 * HD, HD)
            do2, delta = scaled_grad(i, h)
            acc = jnp.zeros((HD, 2 * HD), F32)
            for n in range(PKEYS // CHUNK):
                rows = slice(n * CHUNK, (n + 1) * CHUNK)
                acc = acc + back_chunk(h, rows, wbuf[i, h, rows, :], gbuf[i, h, rows, :], q2, do2, delta)
            dqacc[h] = acc

        @pl.when(i < 2)
        def _():
            for h in range(2):
                q2 = qall[pl.ds(2 * i, 2), h].reshape(2 * HD, HD)
                do2, delta = scaled_grad(i, h)
                dqacc[h] = dqacc[h] + back_chunk(
                    h, slice(PKEYS, KEYS), wresp[i, h], gresp[i, h], q2, do2, delta)

        for h in range(2):
            emit_dq(i, h, dqacc[h])

        @pl.when(i > 0)
        def _():
            send_dq(2 * i)

        send_dq(2 * i + 1)
        return carry

    lax.fori_loop(0, PAIRS, backward_step, 0)

    def grad_swap(n):
        return pltpu.make_async_remote_copy(
            src_ref=gsend.at[n], dst_ref=grecv.at[n], send_sem=g_s.at[n], recv_sem=g_r.at[n],
            device_id=(sibling, z), device_id_type=MESH)

    for n, (acc, scale) in enumerate(((dkacc, 1.0 / 12.0), (dvacc, 1.0))):
        for h in range(2):
            gsend[2 * n + h, 0:512, :] = (acc[h, pl.ds(sib_p, 512), :] * scale).astype(BF16)
            gsend[2 * n + h, 512:, :] = (acc[h, pl.ds(sib_r, ROWS), :] * scale).astype(BF16)
            grad_swap(2 * n + h).start()

    dhall[0] = dhg[chip]

    def wait_proj(s, carry):
        plane_wait_recv(atall.at[0], atall, at_s, at_r, s)
        plane_wait_recv(dhall.at[0], dhall, dh_s, dh_r, s)
        return carry

    lax.fori_loop(1, CHIPS, wait_proj, 0)
    features = dhall[...].reshape(CHIPS * ROWS, JCOLS)
    halves = []
    for n in range(QCOLS // HD):
        rows = slice(n * HD, (n + 1) * HD)
        part = dot_tn(atall[:, :, rows].reshape(CHIPS * ROWS, HD), features)
        low, high = part[:, :DCOLS], part[:, DCOLS:]
        dowsend[rows, :] = jnp.where(core == 0, high, low)
        dow_out[rows, :] = jnp.where(core == 0, low, high)
    dow_swap = pltpu.make_async_remote_copy(
        src_ref=dowsend, dst_ref=dowrecv, send_sem=dw_s, recv_sem=dw_r,
        device_id=(sibling, z), device_id_type=MESH)
    dow_swap.start()

    def add_hidden(dz, total):
        src = lax.rem(z + dz, NZ)
        pltpu.make_async_remote_copy(
            src_ref=hsend.at[src], dst_ref=hrecv.at[src], send_sem=h_s.at[dz], recv_sem=h_r.at[src],
            device_id=(c, src), device_id_type=MESH).wait_recv()
        return total + hrecv[src].astype(F32)

    hidden_out[...] = lax.fori_loop(1, NZ, add_hidden, hsend[z].astype(F32)).astype(BF16)

    for n, (acc, scale, prompt_out, resp_out) in enumerate(
        ((dkacc, 1.0 / 12.0, dpk_out, drk_out), (dvacc, 1.0, dpv_out, drv_out))):
        for h in range(2):
            grad_swap(2 * n + h).wait()
            cols = slice(h * HD, (h + 1) * HD)
            prompt_out[:, cols] = (
                acc[h, pl.ds(own_p, 512), :] * scale + grecv[2 * n + h, 0:512, :].astype(F32)).astype(BF16)
            resp_out[:, cols] = (
                acc[h, pl.ds(own_r, ROWS), :] * scale + grecv[2 * n + h, 512:, :].astype(F32)).astype(BF16)

    def add_dq(s, total):
        plane_wait_recv(dqsend.at[s], dqrecv, dq_s, dq_r, s)
        return total + dqrecv[s].astype(F32)

    query_grad = lax.fori_loop(1, CHIPS, add_dq, dqsend[0].astype(F32))
    for h in range(2):
        rows_first = transpose(query_grad[h] * (1.0 / 12.0)).astype(BF16)
        for g in range(2):
            dq_out[:, (2 * h + g) * HD:(2 * h + g + 1) * HD] = rows_first[g * ROWS:(g + 1) * ROWS, :]

    dow_swap.wait()
    dow_out[...] += dowrecv[...]

    def finish(s, carry):
        plane_copy(qall.at[0], qall, q_s, q_r, s).wait_send()
        plane_copy(doall.at[0], doall, do_s, do_r, s).wait_send()
        plane_copy(osend.at[s], orecv, o_s, o_r, s).wait_send()
        plane_copy(stall.at[0], stall, st_s, st_r, s).wait_send()
        plane_copy(atall.at[0], atall, at_s, at_r, s).wait_send()
        plane_copy(dhg.at[peer_chip(s)], dhall, dh_s, dh_r, s).wait_send()
        plane_copy(dqsend.at[s], dqrecv, dq_s, dq_r, s).wait_send()
        return carry

    lax.fori_loop(1, CHIPS, finish, 0)

    def finish_z(dz, carry):
        block = dhg.at[pl.ds(2 * z, 2)]
        z_copy(block, block, zg_s, zg_r, dz).wait_send()
        z_copy(hsend.at[lax.rem(z + dz, NZ)], hrecv.at[z], h_s, h_r, dz).wait_send()
        return carry

    lax.fori_loop(1, NZ, finish_z, 0)
    for n, (src, dst) in enumerate(kv_pieces()):
        pltpu.make_async_remote_copy(
            src_ref=src, dst_ref=dst, send_sem=kv_s.at[n], recv_sem=kv_r.at[n],
            device_id=(sibling, z), device_id_type=MESH).wait_send()


def per_device(resp_query, resp_key, resp_value, prompt_key, prompt_value, o_weight, d_hidden,
               prompt_offsets, resp_lengths):
    smem = pl.BlockSpec(memory_space=pltpu.SMEM)
    vmem = pl.BlockSpec(memory_space=pltpu.VMEM)
    hbm = pl.BlockSpec(memory_space=pl.ANY)
    shape = jax.ShapeDtypeStruct
    sems = pltpu.SemaphoreType.DMA
    return pl.pallas_call(
        kernel,
        out_shape=(
            shape((ROWS, QCOLS), BF16), shape((ROWS, ZCOLS), BF16), shape((ROWS, QCOLS), BF16),
            shape((512, 2 * HD), BF16), shape((512, 2 * HD), BF16),
            shape((ROWS, 2 * HD), BF16), shape((ROWS, 2 * HD), BF16), shape((QCOLS, DCOLS), F32)),
        in_specs=[smem, smem, vmem, vmem, hbm, hbm, hbm, hbm, hbm],
        out_specs=[vmem] * 8,
        scratch_shapes=[
            pltpu.VMEM((CHIPS, 2, HD, HD), BF16),
            pltpu.VMEM((CHIPS, 2, HD, HD), BF16),
            pltpu.VMEM((2, KEYS, HD), BF16),
            pltpu.VMEM((2, KEYS, HD), BF16),
            pltpu.VMEM((2, HD, KEYS), BF16),
            pltpu.VMEM((2, HD + 16, KEYS), BF16),
            pltpu.VMEM((PAIRS, 2, PKEYS, 2 * HD), BF16),
            pltpu.VMEM((PAIRS, 2, PKEYS, 2 * HD), BF16),
            pltpu.VMEM((2, 2, RKEYS, 2 * HD), BF16),
            pltpu.VMEM((2, 2, RKEYS, 2 * HD), BF16),
            pltpu.VMEM((CHIPS, 2, HD + 16, HD), BF16),
            pltpu.VMEM((CHIPS, 2, HD + 16, HD), BF16),
            pltpu.VMEM((CHIPS, 8, HD), F32),
            pltpu.VMEM((CHIPS, ROWS, QCOLS), BF16),
            pltpu.VMEM((CHIPS, ROWS, JCOLS), BF16),
            pltpu.VMEM((ROWS, WIDTH), F32),
            pltpu.VMEM((CHIPS, ROWS, JCOLS), BF16),
            pltpu.VMEM((QCOLS, WIDTH), BF16),
            pltpu.VMEM((ROWS, WIDTH), F32),
            pltpu.VMEM((NZ, ROWS, ZCOLS), BF16),
            pltpu.VMEM((NZ, ROWS, ZCOLS), BF16),
            pltpu.VMEM((CHIPS, 2, HD, HD), BF16),
            pltpu.VMEM((CHIPS, 2, HD, HD), BF16),
            pltpu.VMEM((2, KEYS, HD), F32),
            pltpu.VMEM((2, KEYS, HD), F32),
            pltpu.VMEM((4, KEYS // 2, HD), BF16),
            pltpu.VMEM((4, KEYS // 2, HD), BF16),
            pltpu.VMEM((QCOLS, DCOLS), F32),
            pltpu.VMEM((QCOLS, DCOLS), F32),
            pltpu.VMEM((2, HD + 16, 2 * HD), F32),
            pltpu.VMEM((2, HD, 2 * HD), F32),
        ] + [sems((CHIPS,))] * 14 + [sems((NZ,))] * 4 + [
            sems((8,)), sems((8,)), sems((8,)), sems, sems((4,)), sems((4,)), sems, sems],
        compiler_params=pltpu.CompilerParams(
            collective_id=0, has_side_effects=True, vmem_limit_bytes=56 * 1024 * 1024),
        cost_estimate=pl.CostEstimate(flops=10 ** 10, bytes_accessed=10 ** 7, transcendentals=10 ** 7),
    )(prompt_offsets, resp_lengths, resp_query, d_hidden, resp_key, resp_value, prompt_key, prompt_value, o_weight)


def solution(mesh):
    both = P("ctx", "tp")
    return jax.shard_map(
        per_device, mesh=mesh,
        in_specs=(both, both, both, both, both, P("tp", None), both, P(), P()),
        out_specs=(both, both, both, both, both, both, both, P("tp", "ctx")),
        check_vma=False)
```

time: 640 us -> 105 us (0.16)
  waiting for transfers between devices: 329 us -> 0 us
  blocking collectives: 159 us -> 0 us
  Pallas kernels: 0 us -> 90.7 us
  matrix products: 55.2 us -> 0 us
  local copies, waits for them, and re-layouts: 52.9 us -> 12.5 us
  other arithmetic: 22.1 us -> 0 us
  between operations: 14.4 us -> 0.65 us
    reduce_scatter x3 -> x0, waiting for transfers between devices: 258 us -> none  [the longest x1 105 us: per_device(): lax.psum_scatter(weight_terms, 'ctx', scatter_dimension=1, tiled=True)]
    psum x1 -> x0, blocking collectives: 109 us -> none  [per_device(): all_totals = lax.psum(totals.reshape(total_rows, q_heads), 'ctx')]
    pallas_call x0 -> x1, Pallas kernels: none -> 90.7 us  [per_device(): pl.pallas_call(kernel, out_shape=(shape((ROWS, QCOLS), BF16), shape((ROWS...]
    all_gather x2 -> x0, waiting for transfers between devices: 70.3 us -> none  [the longest x1 51.1 us: per_device(): all_queries = lax.all_gather(resp_query, 'ctx', axis=0, tiled=True)]
    all_gather x2 -> x0, blocking collectives: 49.9 us -> none  [the longest x1 27.2 us: per_device(): full_grad = lax.all_gather(d_hidden, 'tp', axis=1, tiled=True)]
    dot_general x30 -> x0, matrix products: 49.6 us -> none  [the longest x4 11.7 us: local_backward(): jnp.einsum('qhgd,khd->hgqk', grad_four, value_three, preferred_element_ty...]
    dynamic_slice x32 -> x0, local copies, waits for them, and re-layouts: 18.7 us -> none  [the longest x24 18.5 us: per_device(): lax.scan(forward_block, jnp.int32(0), (block_ids, all_queries.reshape(RES...]
    dynamic_update_slice x20 -> x0, local copies, waits for them, and re-layouts: 11.2 us -> none  [per_device(): lax.scan(forward_block, jnp.int32(0), (block_ids, all_queries.reshape(RES...]
  transfers between devices with their start and end apart: 6 -> 0, of which waited for: 5 -> 0; matrix products, arithmetic and copies ran while one was open for 13% -> 0% of each run, Pallas kernels for 0% -> 0%
where the time goes in v1:
time: 105 us; the launch traced here: 104 us
  Pallas kernels  90.7 us (86%)
  local copies, waits for them, and re-layouts  12.5 us (12%)
    pallas_call x1, Pallas kernels, per_device(): pl.pallas_call(kernel, out_shape=(shape((ROWS, QCOLS), BF16), shape((ROWS...  90.7 us
    unnamed x7, local copies, waits for them, and re-layouts  10.6 us

profile of v1, /device:TPU:2, one launch (start us, length us, event | category | flops | bytes accessed | tf_op | source)
XLA Modules:
  0.0 103.8 jit_solution(17590820348454288996)
XLA Ops:
  0.6 90.7 %shard_map.152 = (bf16[64,512]{1,0:T(8,128)(2,1)}, bf16[64,576]{1,0:T(8,128)(2,1)}, bf16[64,512]{1,0:T(8,128)(2,1)}, bf16[512,256]{1,0:T(8,128)(2,1)}, bf16[512,...) custom-call(s32[4]{0:T(128)} %off_ref.1, s32[4]{0:T(128)} %len_ref.1, ...), custom_call_target="tpu_custom_call" | custom-call | flops 10000000000 | bytes 10000000 | tf_op jit(solution)/shard_map/pallas_call | solution.py:479
  91.3 1.9 %copy.17 = f32[512,144]{0,1:T(8,128)} copy(f32[512,144]{1,0:T(8,128)} %get-tuple-element.15) | data formatting | bytes 589824 | tf_op jit(solution)/shard_map/pallas_call | solution.py:479
  93.2 1.5 %copy.25 = bf16[64,512]{1,0:T(8,128)(2,1)} copy(bf16[64,512]{1,0:T(8,128)(2,1)} %get-tuple-element.24) | data formatting | bytes 131072
  94.7 1.5 %copy.26 = bf16[64,576]{1,0:T(8,128)(2,1)} copy(bf16[64,576]{1,0:T(8,128)(2,1)} %get-tuple-element.25) | data formatting | bytes 147456
  96.2 1.5 %copy.27 = bf16[64,512]{1,0:T(8,128)(2,1)} copy(bf16[64,512]{1,0:T(8,128)(2,1)} %get-tuple-element.26) | data formatting | bytes 131072
  97.7 1.7 %copy.28 = bf16[512,256]{1,0:T(8,128)(2,1)} copy(bf16[512,256]{1,0:T(8,128)(2,1)} %get-tuple-element.27) | data formatting | bytes 524288
  99.4 1.7 %copy.29 = bf16[512,256]{1,0:T(8,128)(2,1)} copy(bf16[512,256]{1,0:T(8,128)(2,1)} %get-tuple-element.28) | data formatting | bytes 524288
  101.0 1.4 %copy.30 = bf16[64,256]{1,0:T(8,128)(2,1)} copy(bf16[64,256]{1,0:T(8,128)(2,1)} %get-tuple-element.29) | data formatting | bytes 65536
  102.4 1.4 %copy.31 = bf16[64,256]{1,0:T(8,128)(2,1)} copy(bf16[64,256]{1,0:T(8,128)(2,1)} %get-tuple-element.30) | data formatting | bytes 65536

commit v2 on v1

v2 whole, which is shorter than its diff:
```python
import math

import jax
import jax.numpy as jnp
from jax import lax
from jax.experimental import pallas as pl
from jax.experimental.pallas import tpu as pltpu
from jax.sharding import PartitionSpec as P

F32 = jnp.float32
BF16 = jnp.bfloat16
MESH = pl.DeviceIdType.MESH

NX, NY, NZ = 4, 4, 8
CHIPS = NX * NY
PAIRS = CHIPS // 2
HD = 128
ROWS = 64
PKEYS = 1024
RKEYS = 128
KEYS = PKEYS + RKEYS
CHUNK = 256
WIDTH = 4608
ZCOLS = WIDTH // NZ
JCOLS = WIDTH // CHIPS
DCOLS = JCOLS // 2
QCOLS = 512

TANH_IN = 1.0 / 600.0
EXP_IN = 50.0 * math.log2(math.e)


def dot_nt(a, b):
    return lax.dot_general(a, b, (((1,), (1,)), ((), ())), preferred_element_type=F32)


def dot_nn(a, b):
    return lax.dot_general(a, b, (((1,), (0,)), ((), ())), preferred_element_type=F32)


def dot_tn(a, b):
    return lax.dot_general(a, b, (((0,), (0,)), ((), ())), preferred_element_type=F32)


def transpose(a):
    return jnp.swapaxes(a, 0, 1)


def kernel(
    off_ref, len_ref, q_hbm, dh_hbm, rk_hbm, rv_hbm, pk_hbm, pv_hbm, ow_hbm,
    attn_out, hidden_out, dq_out, dpk_out, dpv_out, drk_out, drv_out, dow_out,
    attn_vm, hidden_vm, dq_vm, dpk_vm, dpv_vm, drk_vm, drv_vm, dow_vm,
    qall, doall, kbuf, vbuf, kT, vT, wbuf, gbuf, wresp, gresp,
    osend, orecv, osum, olast, stall, atall, dhg, dfull, dhall, ow, hp, hsend, hrecv,
    dqsend, dqrecv, dqsum, dqlast, dkacc, dvacc, gsend, grecv, dowsend, dowrecv, oacc, dqacc, dhown,
    q_s, q_r, do_s, do_r, at_s, at_r, dh_s, dh_r,
    o1_s, o1_r, o2_s, o2_r, dq1_s, dq1_r, dq2_s, dq2_r, st_s, st_r,
    zu_s, zd_s, zg_r, h_s, h_r, q_l, dh_l, kv_l, kv_s, kv_r, ow_l, g_s, g_r, dw_s, dw_r, out_l,
):
    staged = (attn_vm, hidden_vm, dq_vm, dpk_vm, dpv_vm, drk_vm, drv_vm, dow_vm)
    results = (attn_out, hidden_out, dq_out, dpk_out, dpv_out, drk_out, drv_out, dow_out)

    def leaving(n):
        return pltpu.make_async_copy(staged[n], results[n], out_l.at[n])

    def leave(n):
        leaving(n).start()

    c = lax.axis_index("ctx")
    z = lax.axis_index("tp")
    core = lax.rem(c, 2)
    chip = lax.div(c, 2)
    x = lax.div(chip, NY)
    y = lax.rem(chip, NY)
    sibling = chip * 2 + 1 - core

    xs = [lax.rem(x + d, NX) for d in range(NX)]
    ys = [lax.rem(y + d, NY) for d in range(NY)]

    def at(dx, dy):
        px = xs[dx] if isinstance(dx, int) else lax.rem(x + dx, NX)
        py = ys[dy] if isinstance(dy, int) else lax.rem(y + dy, NY)
        return (px * NY + py) * 2 + core, z

    def place(h, m, n):
        return at(m, n) if h == 0 else at(n, m)

    def inverse(n):
        return (NX - n) % NX if isinstance(n, int) else lax.rem(NX - n, NX)

    def remote(src, dst, send, recv, device):
        return pltpu.make_async_remote_copy(
            src_ref=src, dst_ref=dst, send_sem=send, recv_sem=recv, device_id=device, device_id_type=MESH)

    def pass_first(buf, send, recv, h, way):
        to = NY * inverse(way)
        return remote(buf.at[h, 0], buf.at[h, to], send, recv.at[h, to], place(h, way, 0))

    def pass_second(buf, send, recv, h, m, way):
        to = NY * m + inverse(way)
        return remote(buf.at[h, NY * m], buf.at[h, to], send, recv.at[h, to], place(h, 0, way))

    def arrived(buf, send, recv, h, slot):
        remote(buf.at[h, 0], buf.at[h, slot], send, recv.at[h, slot], (sibling, z)).wait_recv()

    def gather(buf, send, recv, stage):
        if stage:
            for h in range(2):
                arrived(buf, send, recv, h, NY * stage)
        else:
            for way in (2, 1, 3):
                for h in range(2):
                    pass_first(buf, send, recv, h, way).start()
        for way in (2, 1, 3):
            for h in range(2):
                pass_second(buf, send, recv, h, stage, way).start()

    def gather_sent(buf, send, recv):
        blocks = buf.at[:, pl.ds(1, CHIPS - 1)]
        remote(blocks, blocks, send, recv.at[0, 0], (sibling, z)).wait_send()

    def sum_first(src, first, send, recv, h, m):
        return remote(src.at[h, m], first.at[h, inverse(m)], send, recv.at[h, inverse(m)], place(h, m, 0))

    def sum_second(mid, last, send, recv, h, n):
        return remote(mid.at[h, n], last.at[h, inverse(n)], send, recv.at[h, inverse(n)], place(h, 0, n))

    def sum_arrived(buf, send, recv, h, m):
        remote(buf.at[h, m], buf.at[h, m], send, recv.at[h, m], place(h, m, 0)).wait_recv()

    def sum_sent(src, mid, send1, recv1, send2, recv2):
        for buf, send, recv in ((src, send1, recv1), (mid, send2, recv2)):
            blocks = buf.at[:, pl.ds(1, NX - 1)]
            remote(blocks, blocks, send, recv.at[0, 0], (sibling, z)).wait_send()

    def z_copy(src, dst, send, recv, dz):
        return remote(src, dst, send.at[dz], recv.at[z], (c, lax.rem(z + dz, NZ)))

    own_p = pl.multiple_of(core * 512, 512)
    own_r = pl.multiple_of(PKEYS + core * ROWS, ROWS)
    sib_p = pl.multiple_of(512 - core * 512, 512)
    sib_r = pl.multiple_of(PKEYS + ROWS - core * ROWS, ROWS)

    def kv_pieces():
        pieces = []
        for h in range(2):
            cols = pl.ds(HD * h, HD)
            pieces.append((pk_hbm.at[:, cols], kbuf.at[h, pl.ds(own_p, 512)]))
            pieces.append((pv_hbm.at[:, cols], vbuf.at[h, pl.ds(own_p, 512)]))
            pieces.append((rk_hbm.at[:, cols], kbuf.at[h, pl.ds(own_r, ROWS)]))
            pieces.append((rv_hbm.at[:, cols], vbuf.at[h, pl.ds(own_r, ROWS)]))
        return pieces

    def kv_landing():
        places = []
        for h in range(2):
            places.append(kbuf.at[h, pl.ds(sib_p, 512)])
            places.append(vbuf.at[h, pl.ds(sib_p, 512)])
            places.append(kbuf.at[h, pl.ds(sib_r, ROWS)])
            places.append(vbuf.at[h, pl.ds(sib_r, ROWS)])
        return places

    barrier = pltpu.get_barrier_semaphore()

    for s in range(1, CHIPS):
        pl.semaphore_signal(barrier, inc=1, device_id=at(s // NY, s % NY), device_id_type=MESH)
    for dz in range(1, NZ):
        pl.semaphore_signal(barrier, inc=1, device_id=(c, lax.rem(z + dz, NZ)), device_id_type=MESH)
    pl.semaphore_signal(barrier, inc=1, device_id=(sibling, z), device_id_type=MESH)

    q_loads = []
    for h in range(2):
        for g in range(2):
            q_loads.append(pltpu.make_async_copy(
                q_hbm.at[:, pl.ds((2 * h + g) * HD, HD)], qall.at[h, 0, pl.ds(g * ROWS, ROWS)], q_l.at[2 * h + g]))
    dh_load = pltpu.make_async_copy(dh_hbm, dhown, dh_l)
    ow_load = pltpu.make_async_copy(ow_hbm, ow, ow_l)
    for copy in q_loads:
        copy.start()
    dh_load.start()
    for n, (src, dst) in enumerate(kv_pieces()):
        pltpu.make_async_copy(src, dst, kv_l.at[n]).start()
    ow_load.start()
    dkacc[...] = jnp.zeros_like(dkacc)
    dvacc[...] = jnp.zeros_like(dvacc)
    dh_load.wait()
    dh_own = dhown[...].astype(F32)
    for half in range(2):
        dhg[2 * z + half] = dh_own[:, half * JCOLS:(half + 1) * JCOLS].astype(BF16)
    for copy in q_loads:
        copy.wait()
    pl.semaphore_wait(barrier, CHIPS - 1 + NZ - 1 + 1)

    def z_at(dz):
        return lax.rem(z + dz + NZ, NZ)

    def chain(k):
        copies = []
        for way, sems_at in ((1, zu_s), (-1, zd_s)):
            src = z_at(-way * k)
            if k < 3:
                block, sem = dhg.at[pl.ds(2 * src, 2)], zg_r.at[src]
            elif way == 1:
                block, sem = dhg.at[pl.ds(2 * src, 1)], zg_r.at[src]
            else:
                block, sem = dhg.at[pl.ds(2 * src + 1, 1)], zg_r.at[NZ + src]
            copies.append(remote(block, block, sems_at.at[k], sem, (c, z_at(way))))
        return copies

    def chain_arrived(k):
        for way, sems_at in ((1, zu_s), (-1, zd_s)):
            src = z_at(-way * k)
            if k < 4:
                block, sem = dhg.at[pl.ds(2 * src, 2)], zg_r.at[src]
            elif way == 1:
                block, sem = dhg.at[pl.ds(2 * src, 1)], zg_r.at[src]
            else:
                block, sem = dhg.at[pl.ds(2 * src + 1, 1)], zg_r.at[NZ + src]
            remote(block, block, sems_at.at[0], sem, (c, z_at(way))).wait_recv()

    def chain_start(k):
        for copy in chain(k):
            copy.start()

    gather(qall, q_s, q_r, 0)
    chain_start(0)
    for n, (src, dst) in enumerate(kv_pieces()):
        remote(src, dst, kv_s.at[n], kv_r.at[n], (sibling, z)).start()

    for n, (src, dst) in enumerate(kv_pieces()):
        pltpu.make_async_copy(src, dst, kv_l.at[n]).wait()
    for n, dst in enumerate(kv_landing()):
        remote(dst, dst, kv_s.at[n], kv_r.at[n], (sibling, z)).wait_recv()
    for h in range(2):
        vT[h, HD:, :] = jnp.ones((16, KEYS), BF16)
        for n in range(KEYS // HD):
            rows = pl.ds(n * HD, HD)
            kT[h, :, rows] = transpose(kbuf[h, rows, :])
            vT[h, 0:HD, rows] = transpose(vbuf[h, rows, :])
    for stage in (1, 2, 3):
        gather(qall, q_s, q_r, stage)

    def major(i):
        return lax.rem(lax.div(i + 1, 2), NX)

    def first_n(i):
        return 2 * lax.rem(i, 2)

    sub = lax.broadcasted_iota(jnp.int32, (CHUNK, 2 * HD), 0)
    lanes_at = lax.broadcasted_iota(jnp.int32, (1, 2 * HD), 1)

    def weigh(s, mask):
        t = jnp.tanh(s * TANH_IN)
        w = jnp.exp2(t * EXP_IN)
        w = jnp.where(mask, w, 0.0)
        return w.astype(BF16), (w * (1.0 - t * t)).astype(BF16)

    def totals_tail(tot):
        rest = tot - tot.astype(BF16).astype(F32)
        row = lax.broadcasted_iota(jnp.int32, tot.shape, 0)
        return jnp.where(row < 8, tot, rest).astype(BF16)

    def emit_o(i, h, acc):
        tail = totals_tail(acc[HD:, :])
        head = acc[:HD, :].astype(BF16)
        for e in range(2):
            lanes = slice(e * HD, (e + 1) * HD)
            osend[h, major(i), first_n(i) + e, 0:HD, :] = head[:, lanes]
            osend[h, major(i), first_n(i) + e, HD:, :] = tail[:, lanes]

    def wait_gathered(i, buf, send, recv):
        slot = NY * major(i) + first_n(i)

        @pl.when(lax.rem(i, 2) == 1)
        def _():
            for h in range(2):
                arrived(buf, send, recv, h, slot)

        for h in range(2):
            arrived(buf, send, recv, h, slot + 1)

    def at_step(i, k, work):
        @pl.when(i == k)
        def _():
            work()

    def resp_step(i, h):
        return (lax.rem(i, 7) == 0, lax.div(i, 7)) if h == 0 else (lax.rem(i, 2) == 0, lax.div(i, 2))

    position = y * RKEYS + core * ROWS

    def chain_on(k):
        chain_arrived(k)
        chain_start(k)

    def project():
        chain_arrived(4)
        for j in range(CHIPS):
            dfull[:, j * JCOLS:(j + 1) * JCOLS] = dhg[j].astype(F32)
        ow_load.wait()
        grad = dot_nt(dfull[...].astype(BF16), ow[...])
        row_at = lax.broadcasted_iota(jnp.int32, (ROWS, QCOLS), 0) + position
        grad = jnp.where(row_at < len_ref[x], grad, 0.0).astype(BF16)
        for h in range(2):
            for g in range(2):
                doall[h, 0, g * ROWS:(g + 1) * ROWS, :] = grad[:, (2 * h + g) * HD:(2 * h + g + 1) * HD]
        gather(doall, do_s, do_r, 0)

    def forward_step(i, carry):
        m, n0 = major(i), first_n(i)
        at_step(i, 1, lambda: chain_on(1))
        at_step(i, 3, lambda: chain_on(2))
        at_step(i, 5, lambda: chain_on(3))
        at_step(i, 7, project)
        wait_gathered(i, qall, q_s, q_r)
        for h in range(2):
            if h == 0:
                low = high = off_ref[lax.rem(x + m, NX)] - chip * PKEYS
            else:
                low = off_ref[lax.rem(x + n0, NX)] - chip * PKEYS
                high = off_ref[lax.rem(x + n0 + 1, NX)] - chip * PKEYS
            limit = jnp.where(lanes_at < HD, low, high)
            q2 = qall[h, pl.ds(NY * m + n0, 2)].reshape(2 * HD, HD)
            acc = jnp.zeros((HD + 16, 2 * HD), F32)
            for n in range(PKEYS // CHUNK):
                rows = slice(n * CHUNK, (n + 1) * CHUNK)
                wb, gb = weigh(dot_nt(kbuf[h, rows, :], q2), sub < limit - n * CHUNK)
                wbuf[i, h, rows, :] = wb
                gbuf[i, h, rows, :] = gb
                acc = acc + dot_nn(vT[h, :, rows], wb)
            oacc[h] = acc

        for h in range(2):
            has_resp, slot = resp_step(i, h)

            @pl.when(has_resp)
            def _():
                lane = lax.broadcasted_iota(jnp.int32, (RKEYS, 2 * HD), 1)
                key = lax.broadcasted_iota(jnp.int32, (RKEYS, 2 * HD), 0) + y * RKEYS
                row = lax.rem(lane, ROWS) + core * ROWS
                if h == 0:
                    first = lax.rem(y + n0, NY) * RKEYS
                    second = lax.rem(y + n0 + 1, NY) * RKEYS
                    mask = key <= row + jnp.where(lane < HD, first, second)
                else:
                    mask = (key <= row + lax.rem(y + m, NY) * RKEYS) & (lane < HD)
                mask = mask & (key < len_ref[x])
                q2 = qall[h, pl.ds(NY * m + n0, 2)].reshape(2 * HD, HD)
                wb, gb = weigh(dot_nt(kbuf[h, PKEYS:, :], q2), mask)
                wresp[h, slot] = wb
                gresp[h, slot] = gb
                oacc[h] = oacc[h] + dot_nn(vT[h, :, PKEYS:], wb)

        for h in range(2):
            emit_o(i, h, oacc[h])

        @pl.when((lax.rem(i, 2) == 0) & (i > 0))
        def _():
            for h in range(2):
                sum_first(osend, orecv, o1_s, o1_r, h, m).start()

        return carry

    lax.fori_loop(0, PAIRS, forward_step, 0)

    def first_sum(src, first, send, recv, h, n):
        total = src[h, 0, n].astype(F32)
        for m in range(1, NX):
            total = total + first[h, m, n].astype(F32)
        return total

    def last_sum(mid, last, h):
        total = mid[h, 0].astype(F32)
        for n in range(1, NX):
            total = total + last[h, n].astype(F32)
        return total

    for h in range(2):
        for m in range(1, NX):
            sum_arrived(orecv, o1_s, o1_r, h, m)
        for n in (1, 2, 3, 0):
            total = first_sum(osend, orecv, o1_s, o1_r, h, n)
            tot = total[HD:HD + 8, :] + total[HD + 8:, :]
            osum[h, n, 0:HD, :] = total[:HD, :].astype(BF16)
            osum[h, n, HD:, :] = totals_tail(jnp.concatenate([tot, tot], axis=0))
            if n:
                sum_second(osum, olast, o2_s, o2_r, h, n).start()

    lane = lax.broadcasted_iota(jnp.int32, (HD, HD), 1)
    valid = lax.rem(lane, ROWS) + position < len_ref[x]
    stall[0] = jnp.zeros((8, HD), F32)
    for h in range(2):
        for n in range(1, NX):
            sum_arrived(olast, o2_s, o2_r, h, n)
        merged = last_sum(osum, olast, h)
        inv = 1.0 / (merged[HD:HD + 1, :] + merged[HD + 8:HD + 9, :])
        own = jnp.where(valid, merged[0:HD, :] * inv, 0.0).astype(BF16).astype(F32)
        grad_t = transpose(doall[h, 0].astype(F32))
        delta = jnp.sum(own * grad_t, axis=0, keepdims=True)
        stall[0, 2 * h:2 * h + 1, :] = inv
        stall[0, 2 * h + 1:2 * h + 2, :] = delta * inv
        rows_first = transpose(own).astype(BF16)
        for g in range(2):
            atall[h, 0, :, g * HD:(g + 1) * HD] = rows_first[g * ROWS:(g + 1) * ROWS, :]

    def direct(src, buf, send, recv, s):
        dx, dy = s // NY, s % NY
        return remote(src, buf.at[NY * inverse(dx) + inverse(dy)], send, recv, at(dx, dy))

    def direct_all(buf, send, recv):
        blocks = buf.at[pl.ds(1, CHIPS - 1)]
        return remote(blocks, blocks, send, recv, (sibling, z))

    def dh_block(s):
        j = xs[s // NY] * NY + ys[s % NY]
        return dhg.at[j]

    for s in range(1, CHIPS):
        direct(stall.at[0], stall, st_s, st_r, s).start()
    for stage in (1, 2, 3):
        gather(doall, do_s, do_r, stage)
    for h in range(2):
        attn_vm[:, h * 2 * HD:(h + 1) * 2 * HD] = atall[h, 0]
    leave(0)

    def send_dh2():
        for s in range(1, CHIPS):
            direct(dh_block(s), dhall, dh_s, dh_r, s).start()

    hp[...] = dot_nn(attn_vm[...], ow[...])
    for n in range(NZ):
        hsend[n] = hp[:, n * ZCOLS:(n + 1) * ZCOLS].astype(BF16)

    def send_h(dz, carry):
        z_copy(hsend.at[lax.rem(z + dz, NZ)], hrecv.at[z], h_s, h_r, dz).start()
        return carry

    lax.fori_loop(1, NZ, send_h, 0)

    direct_all(stall, st_s, st_r).wait_recv()

    def scaled_grad(i, h):
        m, n0 = major(i), first_n(i)
        parts, deltas = [], []
        for e in range(2):
            stats = stall[NY * m + n0 + e] if h == 0 else stall[NY * (n0 + e) + m]
            inv = transpose(jnp.broadcast_to(stats[2 * h:2 * h + 1, :], (HD, HD)))
            parts.append((doall[h, NY * m + n0 + e].astype(F32) * inv).astype(BF16))
            deltas.append(stats[2 * h + 1:2 * h + 2, :])
        return jnp.concatenate(parts, axis=0), jnp.concatenate(deltas, axis=1)

    def back_chunk(h, rows, wb, gb, q2, do2, delta):
        dp = dot_nt(vbuf[h, rows, :], do2)
        ds = (gb.astype(F32) * (dp - delta)).astype(BF16)
        dkacc[h, rows, :] += dot_nn(ds, q2)
        dvacc[h, rows, :] += dot_nn(wb, do2)
        return dot_nn(kT[h, :, rows], ds)

    def backward_step(t, carry):
        i = lax.rem(t + 1, PAIRS)
        at_step(t, 0, lambda: gather(atall, at_s, at_r, 0))
        at_step(t, 2, send_dh2)
        for stage in (1, 2, 3):
            at_step(t, 2 + stage, lambda stage=stage: gather(atall, at_s, at_r, stage))
        m, n0 = major(i), first_n(i)
        wait_gathered(i, doall, do_s, do_r)
        for h in range(2):
            q2 = qall[h, pl.ds(NY * m + n0, 2)].reshape(2 * HD, HD)
            do2, delta = scaled_grad(i, h)
            acc = jnp.zeros((HD, 2 * HD), F32)
            for n in range(PKEYS // CHUNK):
                rows = slice(n * CHUNK, (n + 1) * CHUNK)
                acc = acc + back_chunk(h, rows, wbuf[i, h, rows, :], gbuf[i, h, rows, :], q2, do2, delta)
            dqacc[h] = acc

        for h in range(2):
            has_resp, slot = resp_step(i, h)

            @pl.when(has_resp)
            def _():
                q2 = qall[h, pl.ds(NY * m + n0, 2)].reshape(2 * HD, HD)
                do2, delta = scaled_grad(i, h)
                dqacc[h] = dqacc[h] + back_chunk(
                    h, slice(PKEYS, KEYS), wresp[h, slot], gresp[h, slot], q2, do2, delta)

        for h in range(2):
            for e in range(2):
                dqsend[h, m, n0 + e] = dqacc[h, :, e * HD:(e + 1) * HD].astype(BF16)

        @pl.when((lax.rem(i, 2) == 0) & (i > 0))
        def _():
            for h in range(2):
                sum_first(dqsend, dqrecv, dq1_s, dq1_r, h, m).start()

        return carry

    lax.fori_loop(0, PAIRS, backward_step, 0)

    def grad_swap(n):
        return remote(gsend.at[n], grecv.at[n], g_s.at[n], g_r.at[n], (sibling, z))

    for n, (acc, scale) in enumerate(((dkacc, 1.0 / 12.0), (dvacc, 1.0))):
        for h in range(2):
            gsend[2 * n + h, 0:512, :] = (acc[h, pl.ds(sib_p, 512), :] * scale).astype(BF16)
            gsend[2 * n + h, 512:, :] = (acc[h, pl.ds(sib_r, ROWS), :] * scale).astype(BF16)
            grad_swap(2 * n + h).start()

    for h in range(2):
        for m in range(1, NX):
            sum_arrived(dqrecv, dq1_s, dq1_r, h, m)
        for n in (1, 2, 3, 0):
            dqsum[h, n] = first_sum(dqsend, dqrecv, dq1_s, dq1_r, h, n).astype(BF16)
            if n:
                sum_second(dqsum, dqlast, dq2_s, dq2_r, h, n).start()

    dhall[0] = dhg[chip]

    direct_all(dhall, dh_s, dh_r).wait_recv()
    for h in range(2):
        for m in range(NX):
            for n in range(1, NX):
                arrived(atall, at_s, at_r, h, NY * m + n)
    for h in range(2):
        blocks = []
        for m in range(NX):
            for n in range(NX):
                blocks.append(dhall[NY * m + n] if h == 0 else dhall[NY * n + m])
        features = jnp.concatenate(blocks, axis=0)
        cols = slice(h * 2 * HD, (h + 1) * 2 * HD)
        part = dot_tn(features, atall[h].reshape(CHIPS * ROWS, 2 * HD))
        low, high = part[:DCOLS, :], part[DCOLS:, :]
        dowsend[:, cols] = jnp.where(core == 0, high, low)
        dow_vm[:, cols] = jnp.where(core == 0, low, high)
    dow_swap = remote(dowsend, dowrecv, dw_s, dw_r, (sibling, z))
    dow_swap.start()

    def add_hidden(dz, total):
        src = lax.rem(z + dz, NZ)
        remote(hsend.at[src], hrecv.at[src], h_s.at[dz], h_r.at[src], (c, src)).wait_recv()
        return total + hrecv[src].astype(F32)

    hidden_vm[...] = lax.fori_loop(1, NZ, add_hidden, hsend[z].astype(F32)).astype(BF16)

    leave(1)

    for n, (acc, scale, prompt_out, resp_out) in enumerate(
        ((dkacc, 1.0 / 12.0, dpk_vm, drk_vm), (dvacc, 1.0, dpv_vm, drv_vm))):
        for h in range(2):
            grad_swap(2 * n + h).wait()
            cols = slice(h * HD, (h + 1) * HD)
            prompt_out[:, cols] = (
                acc[h, pl.ds(own_p, 512), :] * scale + grecv[2 * n + h, 0:512, :].astype(F32)).astype(BF16)
            resp_out[:, cols] = (
                acc[h, pl.ds(own_r, ROWS), :] * scale + grecv[2 * n + h, 512:, :].astype(F32)).astype(BF16)
        leave(3 + n)
        leave(5 + n)

    for h in range(2):
        for n in range(1, NX):
            sum_arrived(dqlast, dq2_s, dq2_r, h, n)
        rows_first = transpose(last_sum(dqsum, dqlast, h) * (1.0 / 12.0)).astype(BF16)
        for g in range(2):
            dq_vm[:, (2 * h + g) * HD:(2 * h + g + 1) * HD] = rows_first[g * ROWS:(g + 1) * ROWS, :]

    leave(2)
    dow_swap.wait()
    dow_vm[...] += dowrecv[...]
    leave(7)

    gather_sent(qall, q_s, q_r)
    gather_sent(doall, do_s, do_r)
    gather_sent(atall, at_s, at_r)
    sum_sent(osend, osum, o1_s, o1_r, o2_s, o2_r)
    sum_sent(dqsend, dqsum, dq1_s, dq1_r, dq2_s, dq2_r)

    direct_all(stall, st_s, st_r).wait_send()
    direct_all(dhall, dh_s, dh_r).wait_send()

    def finish_z(dz, carry):
        z_copy(hsend.at[lax.rem(z + dz, NZ)], hrecv.at[z], h_s, h_r, dz).wait_send()
        return carry

    lax.fori_loop(1, NZ, finish_z, 0)
    for k in range(4):
        for copy in chain(k):
            copy.wait_send()
    for n, (src, dst) in enumerate(kv_pieces()):
        remote(src, dst, kv_s.at[n], kv_r.at[n], (sibling, z)).wait_send()
    for n in range(8):
        leaving(n).wait()


def pass_on(*refs):
    for source, target in zip(refs[:8], refs[8:]):
        target[...] = source[...]


def per_device(resp_query, resp_key, resp_value, prompt_key, prompt_value, o_weight, d_hidden,
               prompt_offsets, resp_lengths):
    smem = pl.BlockSpec(memory_space=pltpu.SMEM)
    vmem = pl.BlockSpec(memory_space=pltpu.VMEM)
    hbm = pl.BlockSpec(memory_space=pl.ANY)
    shape = jax.ShapeDtypeStruct
    sems = pltpu.SemaphoreType.DMA
    plane = (NX, NY)
    out_shape = (
        shape((ROWS, QCOLS), BF16), shape((ROWS, ZCOLS), BF16), shape((ROWS, QCOLS), BF16),
        shape((512, 2 * HD), BF16), shape((512, 2 * HD), BF16),
        shape((ROWS, 2 * HD), BF16), shape((ROWS, 2 * HD), BF16), shape((DCOLS, QCOLS), F32))
    results = pl.pallas_call(
        kernel,
        out_shape=out_shape,
        in_specs=[smem, smem, hbm, hbm, hbm, hbm, hbm, hbm, hbm],
        out_specs=[hbm] * 8,
        scratch_shapes=[pltpu.VMEM(o.shape, o.dtype) for o in out_shape] + [
            pltpu.VMEM((2, CHIPS, HD, HD), BF16),
            pltpu.VMEM((2, CHIPS, HD, HD), BF16),
            pltpu.VMEM((2, KEYS, HD), BF16),
            pltpu.VMEM((2, KEYS, HD), BF16),
            pltpu.VMEM((2, HD, KEYS), BF16),
            pltpu.VMEM((2, HD + 16, KEYS), BF16),
            pltpu.VMEM((PAIRS, 2, PKEYS, 2 * HD), BF16),
            pltpu.VMEM((PAIRS, 2, PKEYS, 2 * HD), BF16),
            pltpu.VMEM((2, 4, RKEYS, 2 * HD), BF16),
            pltpu.VMEM((2, 4, RKEYS, 2 * HD), BF16),
            pltpu.VMEM((2,) + plane + (HD + 16, HD), BF16),
            pltpu.VMEM((2,) + plane + (HD + 16, HD), BF16),
            pltpu.VMEM((2, NX, HD + 16, HD), BF16),
            pltpu.VMEM((2, NX, HD + 16, HD), BF16),
            pltpu.VMEM((CHIPS, 8, HD), F32),
            pltpu.VMEM((2, CHIPS, ROWS, 2 * HD), BF16),
            pltpu.VMEM((CHIPS, ROWS, JCOLS), BF16),
            pltpu.VMEM((ROWS, WIDTH), F32),
            pltpu.VMEM((CHIPS, ROWS, JCOLS), BF16),
            pltpu.VMEM((QCOLS, WIDTH), BF16),
            pltpu.VMEM((ROWS, WIDTH), F32),
            pltpu.VMEM((NZ, ROWS, ZCOLS), BF16),
            pltpu.VMEM((NZ, ROWS, ZCOLS), BF16),
            pltpu.VMEM((2,) + plane + (HD, HD), BF16),
            pltpu.VMEM((2,) + plane + (HD, HD), BF16),
            pltpu.VMEM((2, NX, HD, HD), BF16),
            pltpu.VMEM((2, NX, HD, HD), BF16),
            pltpu.VMEM((2, KEYS, HD), F32),
            pltpu.VMEM((2, KEYS, HD), F32),
            pltpu.VMEM((4, KEYS // 2, HD), BF16),
            pltpu.VMEM((4, KEYS // 2, HD), BF16),
            pltpu.VMEM((DCOLS, QCOLS), F32),
            pltpu.VMEM((DCOLS, QCOLS), F32),
            pltpu.VMEM((2, HD + 16, 2 * HD), F32),
            pltpu.VMEM((2, HD, 2 * HD), F32),
            pltpu.VMEM((ROWS, ZCOLS), BF16),
        ] + [sems, sems((2, CHIPS))] * 3 + [sems, sems] + [sems, sems((2, NX))] * 4 + [sems, sems] + [
            sems((4,)), sems((4,)), sems((2 * NZ,)), sems((NZ,)), sems((NZ,)), sems((4,)), sems, sems((8,)), sems((8,)), sems((8,)), sems, sems((4,)), sems((4,)), sems, sems, sems((8,))],
        compiler_params=pltpu.CompilerParams(
            collective_id=0, has_side_effects=True, vmem_limit_bytes=56 * 1024 * 1024),
        cost_estimate=pl.CostEstimate(flops=10 ** 10, bytes_accessed=10 ** 7, transcendentals=10 ** 7),
    )(prompt_offsets, resp_lengths, resp_query, d_hidden, resp_key, resp_value, prompt_key, prompt_value, o_weight)
    results = pl.pallas_call(
        pass_on, out_shape=out_shape, in_specs=[vmem] * 8, out_specs=[vmem] * 8)(*results)
    return results[:7] + (results[7].T,)


def solution(mesh):
    both = P("ctx", "tp")
    return jax.shard_map(
        per_device, mesh=mesh,
        in_specs=(both, both, both, both, both, P("tp", None), both, P(), P()),
        out_specs=(both, both, both, both, both, both, both, P("tp", "ctx")),
        check_vma=False)
```

time: 105 us -> 75.5 us (0.72)
  Pallas kernels: 90.7 us -> 73.8 us
  local copies, waits for them, and re-layouts: 12.5 us -> 0 us
    pallas_call x1 -> x2, Pallas kernels: 90.7 us -> 73.8 us  [the longest x1 71.5 us: per_device(): pl.pallas_call(kernel, out_shape=out_shape, in_specs=[smem, smem, hbm, hb...]
    unnamed x7 -> x0, local copies, waits for them, and re-layouts: 10.6 us -> none
    pallas_call x1 -> x0, local copies, waits for them, and re-layouts: 1.93 us -> none  [per_device(): pl.pallas_call(kernel, out_shape=(shape((ROWS, QCOLS), BF16), shape((ROWS...]
where the time goes in v2:
time: 75.5 us; the launch traced here: 74.4 us
  Pallas kernels  73.8 us (98%)
    pallas_call x1, Pallas kernels, per_device(): pl.pallas_call(kernel, out_shape=out_shape, in_specs=[smem, smem, hbm, hb...  71.5 us
    pallas_call x1, Pallas kernels, per_device(): pl.pallas_call(pass_on, out_shape=out_shape, in_specs=[vmem] * 8, out_spe...  2.25 us

profile of v2, /device:TPU:2, one launch (start us, length us, event | category | flops | bytes accessed | tf_op | source)
XLA Modules:
  0.0 74.4 jit_solution(2969254127845170790)
XLA Ops:
  0.6 71.5 %shard_map.152 = (bf16[64,512]{1,0:T(8,128)(2,1)}, bf16[64,576]{1,0:T(8,128)(2,1)}, bf16[64,512]{1,0:T(8,128)(2,1)}, bf16[512,256]{1,0:T(8,128)(2,1)}, bf16[512,...) custom-call(s32[4]{0:T(128)} %off_ref.1, s32[4]{0:T(128)} %len_ref.1, ...), custom_call_target="tpu_custom_call" | custom-call | flops 10000000000 | bytes 10000000 | tf_op jit(solution)/shard_map/pallas_call | solution.py:610
  72.2 2.3 %shard_map.153 = (bf16[64,512]{1,0:T(8,128)(2,1)}, bf16[64,576]{1,0:T(8,128)(2,1)}, bf16[64,512]{1,0:T(8,128)(2,1)}, bf16[512,256]{1,0:T(8,128)(2,1)}, bf16[512,...) custom-call(bf16[64,512]{1,0:T(8,128)(2,1)} %get-tuple-element.24.refs_0_, ...), custom_call_target="tpu_custom_call" | custom-call | tf_op jit(solution)/shard_map/pallas_call | solution.py:658
